TPU v7x, 128 devices: a whole 4x4x4 slice. The times are simulated.
128 devices in a mesh: wide: 16 (over y, z), grp: 8 (over x, core).
Axes of the slice: x: 4, y: 4, z: 4, core: 2. Of those that a mesh axis runs over, the one named last changes fastest.
Arguments:
- eta_hat: bfloat16 [2, 2048, 2048], P(None, ('wide', 'grp')), may hold values from -0.0008544922 to 0.0008544922
- phi_hat: bfloat16 [2, 2048, 2048], P(None, ('wide', 'grp')), may hold values from -0.00061035156 to 0.00061035156
- patch_tiles: int32 [256], replicated, may hold values from 0 to 1023, as said below
- fraction: bfloat16 [2, 128, 64, 128, 128], P(None, ('wide', 'grp')), may hold values from 0 to 1
Outputs:
- surface: float32 [2048, 2048], P(('wide', 'grp'))
- fraction_next: bfloat16 [2, 128, 64, 128, 128], P(None, ('wide', 'grp'))
- tendency: float32 [2, 2048, 2048], P(None, ('wide', 'grp'))
Inputs may be any that keep to these rules, and one draw needn't show every extreme that they name: `patch_tiles`: for each g below 8, entries g * 32 to (g + 1) * 32 - 1 are distinct tiles, in ascending order, whose column t % 32 lies in [g * 4, (g + 1) * 4). Of these, the tiles of one band (rows (t // 32) // 2 equal) are at most 8, and in every group one band holds exactly 8.
All inputs are finite; a program needn't handle non-finite values.
Results may differ from a plain program's by a relative error of at most 0.019.
Values may be sent and summed in bfloat16 or wider, within the bound.
A program may use at most 192 MiB of HBM per device.

v0:
```python
import math
import jax
import jax.numpy as jnp
from jax import lax
from jax.sharding import PartitionSpec as P

RADIX = 32
TS = 64
Z_BOTTOM = -2.0
Z_TOP = 2.0
DECAY_RATE = 0.5
COURANT = 0.3


def for_sending(shard):

    def short(part):
        return part.astype(jnp.bfloat16) if part.dtype == jnp.float32 else part

    return jax.tree.map(short, shard)


def refine(field):
    return jnp.repeat(jnp.repeat(field, 2, axis=0), 2, axis=1)


def upwind_flux(values, speeds, axis):
    widths = tuple(((1, 1) if dim_index == axis else (0, 0) for dim_index in range(3)))
    padded = jnp.pad(values, widths, mode="edge")
    speed_pad = jnp.pad(speeds, widths, mode="edge")
    count_faces = padded.shape[axis] - 1
    left_vals = lax.slice_in_dim(padded, 0, count_faces, axis=axis)
    right_vals = lax.slice_in_dim(padded, 1, count_faces + 1, axis=axis)
    face_speed = 0.5 * (
        lax.slice_in_dim(speed_pad, 0, count_faces, axis=axis)
        + lax.slice_in_dim(speed_pad, 1, count_faces + 1, axis=axis)
    )
    face_flux = jnp.maximum(face_speed, 0.0) * left_vals + jnp.minimum(face_speed, 0.0) * right_vals
    return lax.slice_in_dim(face_flux, 1, count_faces, axis=axis) - lax.slice_in_dim(
        face_flux, 0, count_faces - 1, axis=axis
    )


def patch_step(state, height, along_x, along_y):
    levels = state.shape[0]
    side = state.shape[1]
    spacing = (Z_TOP - Z_BOTTOM) / levels
    level_z = (Z_BOTTOM + (jnp.arange(levels, dtype=jnp.float32) + 0.5) * spacing)[:, None, None]
    fine_h = refine(height)[None]
    from_sea = jnp.clip((fine_h - level_z) / spacing + 0.5, 0.0, 1.0)
    position = jnp.arange(side, dtype=jnp.float32)
    edge_dist = jnp.minimum(position, side - 1.0 - position)
    distance = jnp.minimum(edge_dist[:, None], edge_dist[None, :])
    weight = 0.3 + 0.7 * jnp.exp(-8.0 * distance / side)
    blended = weight * from_sea + (1.0 - weight) * state.astype(jnp.float32)
    profile = jnp.exp(DECAY_RATE * (level_z - Z_TOP))
    speed_x = refine(along_x)[None] * profile
    speed_y = refine(along_y)[None] * profile
    moved = blended - COURANT * (
        upwind_flux(blended, speed_x, 2) + upwind_flux(blended, speed_y, 1)
    )
    updated = jnp.clip(moved, 0.0, 1.0)
    column = Z_BOTTOM + spacing * jnp.sum(updated, axis=0)
    coarse = column.reshape(side // 2, 2, side // 2, 2).mean(axis=(1, 3))
    return (updated.astype(jnp.bfloat16), coarse)


def small_tables(length):
    index_row = jnp.arange(length, dtype=jnp.int32)
    phase = index_row[:, None] * index_row[None, :] % length
    angle = phase.astype(jnp.float32) * (2.0 * math.pi / length)
    return (jnp.cos(angle).astype(jnp.bfloat16), jnp.sin(angle).astype(jnp.bfloat16))


def contract(data, table, pattern):
    return jnp.einsum(pattern, data, table, preferred_element_type=jnp.float32)


def factored_transform(real_in, imag_in, direction_sign, real_only):
    length = real_in.shape[-1]
    leading = real_in.shape[:-1]
    inner_size = length // RADIX
    cos_p, sin_p = small_tables(RADIX)
    cos_q, sin_q = small_tables(inner_size)
    split_re = real_in.reshape(leading + (RADIX, inner_size))
    segment_re = contract(split_re, cos_p, "...pq,pk->...kq")
    segment_im = direction_sign * contract(split_re, sin_p, "...pq,pk->...kq")
    if imag_in is not None:
        split_im = imag_in.reshape(leading + (RADIX, inner_size))
        segment_re = segment_re - direction_sign * contract(split_im, sin_p, "...pq,pk->...kq")
        segment_im = segment_im + contract(split_im, cos_p, "...pq,pk->...kq")
    first_idx = jnp.arange(RADIX, dtype=jnp.int32)[:, None]
    second_idx = jnp.arange(inner_size, dtype=jnp.int32)[None, :]
    angle = (first_idx * second_idx % length).astype(jnp.float32) * (2.0 * math.pi / length)
    twist_cos = jnp.cos(angle)
    twist_sin = jnp.sin(angle)
    turned_re = (segment_re * twist_cos - direction_sign * segment_im * twist_sin).astype(
        jnp.bfloat16
    )
    turned_im = (segment_im * twist_cos + direction_sign * segment_re * twist_sin).astype(
        jnp.bfloat16
    )
    out_re = contract(turned_re, cos_q, "...kq,qm->...km") - direction_sign * contract(
        turned_im, sin_q, "...kq,qm->...km"
    )
    out_re = jnp.swapaxes(out_re, -1, -2).reshape(leading + (length,))
    if real_only:
        return out_re
    out_im = contract(turned_im, cos_q, "...kq,qm->...km") + direction_sign * contract(
        turned_re, sin_q, "...kq,qm->...km"
    )
    out_im = jnp.swapaxes(out_im, -1, -2).reshape(leading + (length,))
    return (out_re, out_im)


def signed_waves(index_values, length):
    signed = (index_values + length // 2) % length - length // 2
    return signed.astype(jnp.float32) * (2.0 * math.pi / length)


def shards(eta_hat, phi_hat, patch_tiles, fraction):
    row_count = eta_hat.shape[1]
    length = eta_hat.shape[2]
    n_wide = lax.axis_size("wide")
    me_wide = lax.axis_index("wide")
    me_grp = lax.axis_index("grp")
    me_flat = lax.axis_index(("wide", "grp"))
    wave_cols = signed_waves(jnp.arange(length, dtype=jnp.int32), length)
    wave_rows = signed_waves(me_flat * row_count + jnp.arange(row_count, dtype=jnp.int32), length)
    phi_re = phi_hat[0].astype(jnp.float32)
    phi_im = phi_hat[1].astype(jnp.float32)
    real_in = jnp.stack(
        [
            eta_hat[0],
            (-wave_rows[:, None] * phi_im).astype(jnp.bfloat16),
            (-wave_cols[None, :] * phi_im).astype(jnp.bfloat16),
        ]
    )
    imag_in = jnp.stack(
        [
            eta_hat[1],
            (wave_rows[:, None] * phi_re).astype(jnp.bfloat16),
            (wave_cols[None, :] * phi_re).astype(jnp.bfloat16),
        ]
    )
    half_re, half_im = factored_transform(real_in, imag_in, 1.0, False)
    inverse_rows = jnp.swapaxes(
        jnp.concatenate([half_re.astype(jnp.bfloat16), half_im.astype(jnp.bfloat16)]), 1, 2
    )
    turned = lax.all_to_all(inverse_rows, ("wide", "grp"), split_axis=1, concat_axis=2, tiled=True)
    physical = factored_transform(turned[0:3], turned[3:6], 1.0, True)
    band_fields = lax.all_to_all(
        physical.astype(jnp.bfloat16), "grp", split_axis=2, concat_axis=1, tiled=True
    ).astype(physical.dtype)
    band_rows = band_fields.shape[1]
    band_cols = band_fields.shape[2]
    tile_rows = band_rows // TS
    tile_cols = band_cols // TS
    tiles_side = length // TS
    per_group = 2 * n_wide
    group_list = lax.dynamic_slice_in_dim(patch_tiles, me_grp * per_group, per_group)
    row_of = group_list // tiles_side
    col_of = group_list % tiles_side - me_grp * tile_cols
    my_ranks = jnp.arange(2, dtype=jnp.int32) * n_wide + me_wide
    local_t = jnp.arange(tile_rows * tile_cols, dtype=jnp.int32)
    tile_id = (
        (me_wide * tile_rows + local_t // tile_cols) * tiles_side
        + me_grp * tile_cols
        + local_t % tile_cols
    )
    matches = tile_id[:, None] == group_list[None, :]
    active = jnp.any(matches, axis=1)
    rank_index = jnp.sum(
        jnp.where(matches, jnp.arange(per_group, dtype=jnp.int32)[None, :], 0), axis=1
    )
    column_strip = lax.all_gather(
        band_fields.astype(jnp.bfloat16), "wide", axis=1, tiled=True
    ).astype(band_fields.dtype)

    def pick_strip(rank):
        return lax.dynamic_slice(
            column_strip, (0, row_of[rank] * TS, col_of[rank] * TS), (3, TS, TS)
        )

    footprints = jax.vmap(pick_strip)(my_ranks)
    new_states, coarse = jax.vmap(patch_step)(
        fraction[:, 0], footprints[:, 0], footprints[:, 1], footprints[:, 2]
    )
    coarse_flat = coarse.reshape(2, TS * TS)
    every_result = (
        lax.all_gather(
            coarse_flat.reshape(2, 1, TS * TS).astype(jnp.bfloat16), "wide", axis=1, tiled=True
        )
        .astype(jnp.float32)
        .reshape(per_group, TS * TS)
    )
    picked = every_result[rank_index]
    band_tiles = (
        band_fields[0]
        .reshape(tile_rows, TS, tile_cols, TS)
        .transpose(0, 2, 1, 3)
        .reshape(tile_rows * tile_cols, TS * TS)
    )
    corrected = jnp.where(active[:, None], picked, band_tiles)
    surface_band = (
        corrected.reshape(tile_rows, tile_cols, TS, TS)
        .transpose(0, 2, 1, 3)
        .reshape(band_rows, band_cols)
    )
    surface = lax.all_to_all(
        for_sending(surface_band), "grp", split_axis=0, concat_axis=1, tiled=True
    ).astype(surface_band.dtype)
    along_x = physical[1]
    along_y = physical[2]
    drive = (-(surface + 0.5 * (along_x * along_x + along_y * along_y))).astype(jnp.bfloat16)
    drive_re, drive_im = factored_transform(drive, None, -1.0, False)
    pair_rows = jnp.swapaxes(
        jnp.stack([drive_re.astype(jnp.bfloat16), drive_im.astype(jnp.bfloat16)]), 1, 2
    )
    pair_cols = lax.all_to_all(pair_rows, ("wide", "grp"), split_axis=1, concat_axis=2, tiled=True)
    spec_re, spec_im = factored_transform(pair_cols[0], pair_cols[1], -1.0, False)
    tendency = jnp.stack([spec_re, spec_im]) * (1.0 / length)
    return (surface, new_states[:, None], tendency)


def solution(mesh):
    placed = (
        P(None, ("wide", "grp"), None),
        P(None, ("wide", "grp"), None),
        P(),
        P(None, ("wide", "grp"), None, None, None),
    )
    return jax.shard_map(
        shards,
        mesh=mesh,
        in_specs=placed,
        out_specs=(
            P(("wide", "grp"), None),
            P(None, ("wide", "grp"), None, None, None),
            P(None, ("wide", "grp"), None),
        ),
        check_vma=False,
    )
```

profile of v0, /device:TPU:1, one launch (start us, length us, event | category | flops | bytes accessed | tf_op | source)
XLA Modules:
  0.0 338.8 jit_solution(14497222716978649175)
XLA Ops:
  7.4 0.9 fusion.251
  8.4 1.0 fusion.42
  13.8 0.8 convert_element_type.411
  15.0 0.8 convert_element_type.408
  15.9 4.1 %copy.124 = bf16[6,2048,16]{2,0,1:T(8,128)(2,1)} copy(bf16[6,2048,16]{1,2,0:T(8,128)(2,1)S(1)} %maximum_bitcast_fusion) | data formatting | bytes 786432 | tf_op jit(solution)/shard_map/transpose | solution.py:147
  20.0 5.6 %reshape.527 = bf16[128,2,768]{2,1,0:T(2,128)(2,1)S(1)} reshape(bf16[2048,6,16]{2,1,0:T(8,128)(2,1)} %bitcast.240) | data formatting | bytes 786432
  25.6 24.1 %all_to_all.58 = bf16[128,2,768]{2,1,0:T(2,128)(2,1)S(1)} all-to-all(bf16[128,2,768]{2,1,0:T(2,128)(2,1)S(1)} %reshape.527), channel_id=1, replica_groups=mesh['wide'=16,'grp'=8] {'wide','grp'}, dimensions={0} | all-to-all | bytes 786432 | tf_op jit(solution)/shard_map/all_to_all | solution.py:150
  49.7 4.8 %reshape.528 = bf16[2048,6,16]{2,1,0:T(8,128)(2,1)} reshape(bf16[128,2,768]{2,1,0:T(2,128)(2,1)S(1)} %all_to_all.58) | data formatting | bytes 786432
  54.6 6.1 %copy.158 = bf16[6,128,16,16]{2,1,3,0:T(8,128)(2,1)S(1)} copy(bf16[6,128,16,16]{3,0,2,1:T(8,128)(2,1)} %bitcast.239) | data formatting | bytes 786432 | tf_op jit(solution)/shard_map/all_to_all | solution.py:150
  60.7 1.9 fusion.249
  62.6 4.3 %copy.126 = bf16[3,16,128,16]{3,2,1,0:T(8,128)(2,1)S(1)} copy(bf16[3,16,128,16]{1,2,3,0:T(8,128)(2,1)} %get-tuple-element.58) | data formatting | bytes 393216 | tf_op jit(solution)/shard_map/slice | solution.py:151
  67.7 1.2 fusion.99
  69.0 1.3 fusion.106
  70.2 3.1 copy.127
  74.2 1.5 convolution_add_fusion
  75.6 1.5 convolution_subtract_fusion.1
  77.9 3.4 %copy.159 = bf16[3,16,64,32]{1,0,3,2:T(4,128)(2,1)S(1)} copy(bf16[3,16,64,32]{2,3,1,0:T(8,128)(2,1)S(1)} %get-tuple-element.82) | data formatting | bytes 393216 | tf_op jit(solution)/shard_map/convert_element_type | solution.py:153
  81.3 1.9 reshape.529
  83.2 9.3 %all_to_all.59 = bf16[8,2,6144]{2,1,0:T(2,128)(2,1)S(1)} all-to-all(bf16[8,2,6144]{2,1,0:T(2,128)(2,1)S(1)} %reshape.529), channel_id=1, replica_groups=mesh['wide'=16,'grp'=8] {'grp'}, dimensions={0} | all-to-all | bytes 393216 | tf_op jit(solution)/shard_map/all_to_all | solution.py:152
  92.5 2.0 reshape.530
  94.5 2.0 copy.161
  99.9 1.0 copy.160
  101.1 39.6 %all-gather.2.cloned.1.call-done = bf16[3,2048,256]{2,1,0:T(8,128)(2,1)} async-done(((bf16[3,128,256]{2,1,0:T(8,128)(2,1)}), bf16[3,2048,256]{2,1,0:T(8,128)(2,1)}) %all-gather.2.cloned.1.call-update) | async-done | bytes 3145744 | tf_op jit(solution)/shard_map/all_gather | solution.py:176
  140.7 5.1 %convert_element_type.418 = f32[3,2048,256]{2,1,0:T(8,128)} convert(bf16[3,2048,256]{2,1,0:T(8,128)(2,1)} %all-gather.2.cloned.1.call-done) | non-fusion elementwise | flops 1572864 | bytes 9437184 | tf_op jit(solution)/shard_map/convert_element_type | solution.py:178
  145.8 5.9 %while.1 = (s32[]{:T(128)}, f32[3,2048,256]{2,1,0:T(8,128)}, s32[2,3]{1,0:T(2,128)S(1)}, f32[2,3,64,64]{3,2,1,0:T(8,128)S(1)}, s32[]{:T(128)}) while((s32[]{:T(128)}, f32[3,2048,256]{2,1,0:T(8,128)}, s32[2,3]{1,0:T(2,128)S(1)}, f32[2,3,64,64]{3,2,1,0:T(8,128)S(1)}, s32[]{:T(128)}) %tuple.55), condition=%wide.while_cond, body=%wide.while_body.sunk | while | flops 2 | bytes 147581 | solution.py:181
  146.4 2.3 bitcast_dynamic-update-slice_fusion.2
  149.3 2.3 bitcast_dynamic-update-slice_fusion.2
  152.3 0.9 slice_bitcast_fusion.1
  153.6 3.9 %fusion.8 = f32[2,64,128,128]{3,2,1,0:T(8,128)S(1)} fusion(bf16[2,1,64,128,128]{4,3,2,1,0:T(8,128)(2,1)} %param.7, f32[128,128]{1,0:T(8,128)S(1)} %get-tuple-element.81, f32[64]{0:T(128)S(1)} %fusion.129, f32[2,128,128]{2,1,0:T(8,128)S(1)} %copy.134, f32[128,128]{1,0:T(8,128)S(1)} %get-tuple-element.80), kind=kLoop, calls=%fused_computation.22 | loop fusion | flops 16777216 | bytes 12845312 | tf_op jit(solution)/shard_map/vmap()/add | solution.py:55
  157.6 7.7 %fusion.246 = (f32[2,64,128,1]{3,2,1,0:T(8,128)}, f32[2,64,128,1]{3,2,1,0:T(8,128)}) fusion(f32[2,64,128,128]{3,2,1,0:T(8,128)S(1)} %fusion.8), kind=kLoop, calls=%fused_computation.353 | loop fusion | bytes 262144 | tf_op jit(solution)/shard_map/vmap(jit(_pad))/slice | solution.py:29
  166.5 5.4 %broadcast_multiply_fusion.1 = (f32[2,64,128,128]{3,2,1,0:T(8,128)}, f32[2,64,128,128]{3,2,1,0:T(8,128)S(1)}) fusion(f32[64]{0:T(128)S(1)} %multiply_exponential_fusion, f32[2,128,128]{2,1,0:T(8,128)S(1)} %copy.137, f32[2,128,128]{2,1,0:T(8,128)S(1)} %copy.139), kind=kLoop, calls=%fused_computation.25 | loop fusion | flops 4194304 | bytes 17039616 | tf_op jit(solution)/shard_map/vmap()/mul | solution.py:57
  171.9 3.2 copy-done.1
  175.2 13.3 %fusion.245 = (f32[2,64,128,1]{3,2,1,0:T(8,128)}, f32[2,64,128,1]{3,2,1,0:T(8,128)}) fusion(f32[2,64,128,128]{3,2,1,0:T(8,128)} %get-tuple-element.78), kind=kLoop, calls=%fused_computation.352 | loop fusion | bytes 262144 | tf_op jit(solution)/shard_map/vmap(jit(_pad))/slice | solution.py:30
  188.5 12.6 %fusion.3 = f32[2,64,129,128]{3,2,1,0:T(8,128)} fusion(f32[2,64,128,128]{3,2,1,0:T(8,128)S(1)} %bitcast.236, f32[2,64,1,128]{3,2,1,0:T(1,128)S(1)} %get-tuple-element.56, f32[2,64,1,128]{3,2,1,0:T(1,128)S(1)} %get-tuple-element.55, f32[2,64,1,128]{3,2,1,0:T(1,128)S(1)} %get-tuple-element.54, f32[2,64,128,128]{3,2,1,0:T(8,128)} %copy-done.1, ...), kind=kLoop, calls=%fused_computation.13 | loop fusion | flops 23248896 | bytes 25493504 | tf_op jit(solution)/shard_map/vmap()/add | solution.py:38
  201.1 25.7 %fusion.1 = f32[2,64,128,129]{3,2,1,0:T(8,128)} fusion(f32[2,64,128,128]{3,2,1,0:T(8,128)S(1)} %bitcast.236, f32[2,64,128,1]{3,2,1,0:T(8,128)} %get-tuple-element.52, f32[2,64,128,1]{3,2,1,0:T(8,128)} %get-tuple-element.51, f32[2,64,128,1]{3,2,1,0:T(8,128)} %get-tuple-element.50, f32[2,64,128,128]{3,2,1,0:T(8,128)} %get-tuple-element.78, ...), kind=kLoop, calls=%fused_computation.8 | loop fusion | flops 23248896 | bytes 25493504 | tf_op jit(solution)/shard_map/vmap()/add | solution.py:38
  226.8 22.0 %convert_bitcast_fusion = (bf16[2,1,64,128,128]{4,3,2,1,0:T(8,128)(2,1)}, f32[2,64,128,128]{3,2,1,0:T(8,128)}) fusion(f32[2,64,129,128]{3,2,1,0:T(8,128)} %fusion.3, f32[2,64,128,129]{3,2,1,0:T(8,128)} %fusion.1, bf16[2,1,64,128,128]{4,3,2,1,0:T(8,128)(2,1)} %param.7, f32[128,128]{1,0:T(8,128)S(1)} %get-tuple-element.81, f32[64]{0:T(128)S(1)} %fusion.129, ...), kind=kLoop, calls=%fused_computation.23 | loop fusion | flops 31457280 | bytes 50594048 | tf_op jit(solution)/shard_map/broadcast_in_dim | solution.py:223
  248.9 3.8 %reduce_sum.29 = f32[2,128,128]{2,1,0:T(8,128)S(1)} reduce(f32[2,64,128,128]{3,2,1,0:T(8,128)} %get-tuple-element.44, f32[]{:T(128)} %constant.200.clone.1), dimensions={1}, to_apply=%region_1.2 | reduce | flops 2064384 | bytes 8519684 | tf_op jit(solution)/shard_map/vmap()/reduce_sum | solution.py:63
  252.7 9.8 %add.508 = f32[2,64,2,64,2]{4,3,2,1,0:T(8,128)} reshape(f32[2,128,128]{2,1,0:T(8,128)S(1)} %multiply_add_fusion) | data formatting | bytes 262144 | tf_op jit(solution)/shard_map/vmap()/add | solution.py:63
  262.5 4.5 %reduce_sum.30 = f32[2,64,64]{2,1,0:T(8,128)S(1)} reduce(f32[2,64,2,64,2]{4,3,2,1,0:T(8,128)} %add.508, f32[]{:T(128)} %constant.200.clone.1), dimensions={2,4}, to_apply=%region_2.3 | reduce | flops 24576 | bytes 163844 | tf_op jit(solution)/shard_map/vmap()/reduce_sum | solution.py:64
  267.2 17.1 %all_gather.7 = bf16[2,16,4096]{2,0,1:T(2,128)(2,1)S(1)} all-gather(bf16[2,1,4096]{2,0,1:T(2,128)(2,1)S(1)} %convert_element_type.422), channel_id=1, replica_groups=mesh['wide'=16,'grp'=8] {'wide'}, dimensions={1}, use_global_device_ids=true | all-gather | bytes 278528 | tf_op jit(solution)/shard_map/all_gather | solution.py:191
  286.1 11.0 %all-to-all-start.2 = ((bf16[8,16,256]{2,1,0:T(8,128)(2,1)}), bf16[8,16,256]{2,1,0:T(8,128)(2,1)S(1)}, u32[]{:S(2)}, u32[]{:S(2)}) async-start(bf16[8,16,256]{2,1,0:T(8,128)(2,1)} %convert_element_type.425), calls=%async_computation.2 | async-start | bytes 131072 | tf_op jit(solution)/shard_map/all_to_all | solution.py:210
  297.5 4.4 %all-to-all-done.2 = bf16[8,16,256]{2,1,0:T(8,128)(2,1)S(1)} async-done(((bf16[8,16,256]{2,1,0:T(8,128)(2,1)}), bf16[8,16,256]{2,1,0:T(8,128)(2,1)S(1)}, u32[]{:S(2)}, u32[]{:S(2)}) %all-to-all-start.2) | async-done | bytes 65568 | tf_op jit(solution)/shard_map/all_to_all | solution.py:210
  305.6 1.5 reshape.531
  307.2 4.9 %all-to-all-start.3 = ((bf16[128,2,256]{2,1,0:T(2,128)(2,1)}), bf16[128,2,256]{2,1,0:T(2,128)(2,1)S(1)}, u32[]{:S(2)}, u32[]{:S(2)}) async-start(bf16[128,2,256]{2,1,0:T(2,128)(2,1)} %reshape.531), calls=%async_computation.3 | async-start | bytes 262144 | tf_op jit(solution)/shard_map/all_to_all | solution.py:220
  312.8 9.3 %all-to-all-done.3 = bf16[128,2,256]{2,1,0:T(2,128)(2,1)S(1)} async-done(((bf16[128,2,256]{2,1,0:T(2,128)(2,1)}), bf16[128,2,256]{2,1,0:T(2,128)(2,1)S(1)}, u32[]{:S(2)}, u32[]{:S(2)}) %all-to-all-start.3) | async-done | bytes 131104 | tf_op jit(solution)/shard_map/all_to_all | solution.py:220
  322.7 2.0 copy.162
  324.9 1.1 copy.150
  326.8 1.1 copy.151
  (142 shorter events, 26.0 us)
Async XLA Ops:
  7.2 133.5 %all-gather.2.cloned.1.call-start = ((), (), s32[]{:S(2)}) async-start(), calls=%async_computation.4 | async-start | bytes 3342336 | tf_op jit(solution)/shard_map/all_gather | solution.py:176
  7.3 6.5 %copy-start.3 = (f32[32,64]{1,0:T(8,128)}, f32[32,64]{1,0:T(8,128)S(1)}, u32[]{:S(2)}) copy-start(f32[32,64]{1,0:T(8,128)S(1)} %get-tuple-element.88) | copy-start | bytes 24580
  62.6 7.6 %copy-start.2 = (bf16[3,16,128,16]{1,2,3,0:T(8,128)(2,1)S(1)}, bf16[3,16,128,16]{1,2,3,0:T(8,128)(2,1)}, u32[]{:S(2)}) copy-start(bf16[3,16,128,16]{1,2,3,0:T(8,128)(2,1)} %get-tuple-element.57) | copy-start | bytes 589828
  70.2 6.9 %copy-start.4 = (f32[32,64]{1,0:T(8,128)S(1)}, f32[32,64]{1,0:T(8,128)}, u32[]{:S(2)}) copy-start(f32[32,64]{1,0:T(8,128)} %copy-done.3) | copy-start | bytes 24580
  77.1 19.5 %copy-start.8 = (s32[256]{0:T(256)S(1)}, s32[256]{0:T(256)}, u32[]{:S(2)}) copy-start(s32[256]{0:T(256)} %param.6) | copy-start | bytes 3076
  151.7 0.7 copy-start.5
  157.5 8.4 %copy-start = (f32[2,64,128,128]{3,2,1,0:T(8,128)}, f32[2,64,128,128]{3,2,1,0:T(8,128)S(1)}, u32[]{:S(2)}) copy-start(f32[2,64,128,128]{3,2,1,0:T(8,128)S(1)} %fusion.8) | copy-start | bytes 25165828
  166.4 22.1 %slice-start = ((s8[8388608]{0:T(1024)(128)(4,1)}), s8[4194304]{0:T(1024)(128)(4,1)S(1)}, s32[]{:S(2)}) async-start(s8[8388608]{0:T(1024)(128)(4,1)} %bitcast.235), calls=%async_computation.5 | async-start | bytes 8388608
  171.9 3.2 copy-start.1
  175.2 13.3 %slice-start.1 = ((s8[8388608]{0:T(1024)(128)(4,1)}), s8[4194304]{0:T(1024)(128)(4,1)S(1)}, s32[]{:S(2)}) async-start(s8[8388608]{0:T(1024)(128)(4,1)} %bitcast.235), calls=%async_computation.6 | async-start | bytes 8388608
  252.7 32.5 %copy-start.7 = (pred[2,4]{1,0:T(4,128)(4,1)S(1)}, pred[2,4]{1,0:T(4,128)(4,1)}, u32[]{:S(2)}) copy-start(pred[2,4]{1,0:T(4,128)(4,1)} %broadcast_in_dim.29) | copy-start | bytes 28
  262.5 39.9 %copy-start.6 = (f32[32,64]{1,0:T(8,128)S(1)}, f32[32,64]{1,0:T(8,128)}, u32[]{:S(2)}) copy-start(f32[32,64]{1,0:T(8,128)} %get-tuple-element.93) | copy-start | bytes 24580
  286.1 15.8 %all-to-all-start.2 = ((bf16[8,16,256]{2,1,0:T(8,128)(2,1)}), bf16[8,16,256]{2,1,0:T(8,128)(2,1)S(1)}, u32[]{:S(2)}, u32[]{:S(2)}) async-start(bf16[8,16,256]{2,1,0:T(8,128)(2,1)} %convert_element_type.425), calls=%async_computation.2 | async-start | bytes 131072 | tf_op jit(solution)/shard_map/all_to_all | solution.py:210
  307.2 14.9 %all-to-all-start.3 = ((bf16[128,2,256]{2,1,0:T(2,128)(2,1)}), bf16[128,2,256]{2,1,0:T(2,128)(2,1)S(1)}, u32[]{:S(2)}, u32[]{:S(2)}) async-start(bf16[128,2,256]{2,1,0:T(2,128)(2,1)} %reshape.531), calls=%async_computation.3 | async-start | bytes 262144 | tf_op jit(solution)/shard_map/all_to_all | solution.py:220
Sparse Core Ops, SparseCore 0:
  96.7 44.0 all-gather.1
where the time goes:
time: 346 us; the launch traced here: 339 us
  local copies, waits for them, and re-layouts  104 us (30%)
  other arithmetic  86.5 us (25%)
  waiting for transfers between devices  53.3 us (15%)
  blocking collectives  50.5 us (15%)
  starting transfers between devices  16 us (5%)
  between operations  15.4 us (4%)
  matrix products  13 us (4%)
    all_gather x1, waiting for transfers between devices, shards(): lax.all_gather(band_fields.astype(jnp.bfloat16), 'wide', axis=1, tiled=True)  39.6 us
    add x2, other arithmetic, upwind_flux(): jnp.maximum(face_speed, 0.0) * left_vals  38.3 us
    all_to_all x1, blocking collectives, shards(): lax.all_to_all(inverse_rows, ('wide', 'grp'), split_axis=1, concat_axis=2...  24.1 us
    broadcast_in_dim x1, other arithmetic, shards(): return (surface, new_states[:, None], tendency)  22 us
    unnamed x33, local copies, waits for them, and re-layouts  21.2 us
    all_gather x1, blocking collectives, shards(): lax.all_gather(coarse_flat.reshape(2, 1, TS * TS).astype(jnp.bfloat16), '...  17.1 us
    slice x2, local copies, waits for them, and re-layouts, upwind_flux(): speed_pad = jnp.pad(speeds, widths, mode='edge')  13.4 us
    dot_general x28, matrix products, contract(): return jnp.einsum(pattern, data, table, preferred_element_type=jnp.float32)  13 us
  transfers between devices with their start and end apart: 3, of which 3 were waited for; matrix products, arithmetic and copies ran while one was open for 2% of the time, Pallas kernels for 0%

commit v1 on v0

--- a/solution.py
+++ b/solution.py
@@ -10,6 +10,29 @@
 Z_TOP = 2.0
 DECAY_RATE = 0.5
 COURANT = 0.3
+
+
+def split_up(x, dim, size):
+    lengths = x.shape
+    tiles = x.reshape(*lengths[:dim], size, lengths[dim] // size, *lengths[dim + 1 :])
+    return jnp.moveaxis(tiles, dim, 0)
+
+
+def laid_out(blocks, dim):
+    shape = list(blocks.shape[1:])
+    shape[dim] *= blocks.shape[0]
+    return jnp.moveaxis(blocks, 0, dim).reshape(shape)
+
+
+def exchange_in_pairs(value, axis, split_dim, concat_dim):
+    length, place = (lax.axis_size(axis), lax.axis_index(axis))
+    pieces = split_up(value, split_dim, length)
+    outs = [pieces[place]]
+    for lap in range(1, length):
+        sent = pieces[place ^ lap]
+        outs.append(lax.ppermute(sent, axis, [(i, i ^ lap) for i in range(length)]))
+    pieces = jnp.stack(outs)[place ^ jnp.arange(length)]
+    return laid_out(pieces, concat_dim)
 
 
 def for_sending(shard):
@@ -207,9 +230,7 @@
         .transpose(0, 2, 1, 3)
         .reshape(band_rows, band_cols)
     )
-    surface = lax.all_to_all(
-        for_sending(surface_band), "grp", split_axis=0, concat_axis=1, tiled=True
-    ).astype(surface_band.dtype)
+    surface = exchange_in_pairs(for_sending(surface_band), "grp", 0, 1).astype(surface_band.dtype)
     along_x = physical[1]
     along_y = physical[2]
     drive = (-(surface + 0.5 * (along_x * along_x + along_y * along_y))).astype(jnp.bfloat16)

time: 346 us -> 350 us (1.012)
  starting transfers between devices: 16 us -> 20.7 us
    ppermute x0 -> x7, starting transfers between devices: none -> 14.2 us  [exchange_in_pairs(): outs.append(lax.ppermute(sent, axis, [(i, i ^ lap) for i in range(length)]))]
    all_to_all x1 -> x0, starting transfers between devices: 11 us -> none  [shards(): lax.all_to_all(for_sending(surface_band), 'grp', split_axis=0, concat_axi...]
    ppermute x0 -> x7, waiting for transfers between devices: none -> 4.76 us  [exchange_in_pairs(): outs.append(lax.ppermute(sent, axis, [(i, i ^ lap) for i in range(length)]))]
    all_to_all x1 -> x0, waiting for transfers between devices: 4.4 us -> none  [shards(): lax.all_to_all(for_sending(surface_band), 'grp', split_axis=0, concat_axi...]
    unnamed x33 -> x39, local copies, waits for them, and re-layouts: 21.2 us -> 21.2 us
  transfers between devices with their start and end apart: 3 -> 9, of which waited for: 3 -> 4; matrix products, arithmetic and copies ran while one was open for 2% -> 2% of each run, Pallas kernels for 0% -> 0%
where the time goes in v1:
time: 350 us; the launch traced here: 344 us
  local copies, waits for them, and re-layouts  104 us (30%)
  other arithmetic  87.3 us (25%)
  waiting for transfers between devices  53 us (15%)
  blocking collectives  50.2 us (14%)
  starting transfers between devices  20.7 us (6%)
  between operations  15.2 us (4%)
  matrix products  12.9 us (4%)
    all_gather x1, waiting for transfers between devices, shards(): lax.all_gather(band_fields.astype(jnp.bfloat16), 'wide', axis=1, tiled=True)  38.9 us
    add x2, other arithmetic, upwind_flux(): jnp.maximum(face_speed, 0.0) * left_vals  38.5 us
    all_to_all x1, blocking collectives, shards(): lax.all_to_all(inverse_rows, ('wide', 'grp'), split_axis=1, concat_axis=2...  23.8 us
    broadcast_in_dim x1, other arithmetic, shards(): return (surface, new_states[:, None], tendency)  22 us
    unnamed x39, local copies, waits for them, and re-layouts  21.2 us
    all_gather x1, blocking collectives, shards(): lax.all_gather(coarse_flat.reshape(2, 1, TS * TS).astype(jnp.bfloat16), '...  17.1 us
    ppermute x7, starting transfers between devices, exchange_in_pairs(): outs.append(lax.ppermute(sent, axis, [(i, i ^ lap) for i in range(length)]))  14.2 us
    slice x2, local copies, waits for them, and re-layouts, upwind_flux(): speed_pad = jnp.pad(speeds, widths, mode='edge')  13.4 us
  transfers between devices with their start and end apart: 9, of which 4 were waited for; matrix products, arithmetic and copies ran while one was open for 2% of the time, Pallas kernels for 0%

profile of v1, /device:TPU:1, one launch (start us, length us, event | category | flops | bytes accessed | tf_op | source)
XLA Modules:
  0.0 343.7 jit_solution(17321797187967450919)
XLA Ops:
  15.9 4.1 %copy.124 = bf16[6,2048,16]{2,0,1:T(8,128)(2,1)} copy(bf16[6,2048,16]{1,2,0:T(8,128)(2,1)S(1)} %maximum_bitcast_fusion) | data formatting | bytes 786432 | tf_op jit(solution)/shard_map/transpose | solution.py:170
  20.0 5.6 %reshape.550 = bf16[128,2,768]{2,1,0:T(2,128)(2,1)S(1)} reshape(bf16[2048,6,16]{2,1,0:T(8,128)(2,1)} %bitcast.270) | data formatting | bytes 786432
  25.6 23.8 %all_to_all.48 = bf16[128,2,768]{2,1,0:T(2,128)(2,1)S(1)} all-to-all(bf16[128,2,768]{2,1,0:T(2,128)(2,1)S(1)} %reshape.550), channel_id=1, replica_groups=mesh['wide'=16,'grp'=8] {'wide','grp'}, dimensions={0} | all-to-all | bytes 786432 | tf_op jit(solution)/shard_map/all_to_all | solution.py:173
  49.4 4.8 %reshape.551 = bf16[2048,6,16]{2,1,0:T(8,128)(2,1)} reshape(bf16[128,2,768]{2,1,0:T(2,128)(2,1)S(1)} %all_to_all.48) | data formatting | bytes 786432
  54.3 6.1 %copy.158 = bf16[6,128,16,16]{2,1,3,0:T(8,128)(2,1)S(1)} copy(bf16[6,128,16,16]{3,0,2,1:T(8,128)(2,1)} %bitcast.269) | data formatting | bytes 786432 | tf_op jit(solution)/shard_map/all_to_all | solution.py:173
  60.4 1.9 fusion.250
  62.3 4.3 %copy.126 = bf16[3,16,128,16]{3,2,1,0:T(8,128)(2,1)S(1)} copy(bf16[3,16,128,16]{1,2,3,0:T(8,128)(2,1)} %get-tuple-element.58) | data formatting | bytes 393216 | tf_op jit(solution)/shard_map/slice | solution.py:174
  67.4 1.2 fusion.99
  68.7 1.2 fusion.106
  69.9 3.1 copy.127
  73.8 1.5 convolution_add_fusion
  75.3 1.4 convolution_subtract_fusion.1
  77.6 3.4 copy.159
  81.0 1.9 reshape.552
  82.9 9.3 %all_to_all.49 = bf16[8,2,6144]{2,1,0:T(2,128)(2,1)S(1)} all-to-all(bf16[8,2,6144]{2,1,0:T(2,128)(2,1)S(1)} %reshape.552), channel_id=1, replica_groups=mesh['wide'=16,'grp'=8] {'grp'}, dimensions={0} | all-to-all | bytes 393216 | tf_op jit(solution)/shard_map/all_to_all | solution.py:175
  92.2 2.0 reshape.553
  94.2 2.0 copy.161
  100.3 1.0 copy.160
  101.5 38.9 %all-gather.2.cloned.1.call-done = bf16[3,2048,256]{2,1,0:T(8,128)(2,1)} async-done(((bf16[3,128,256]{2,1,0:T(8,128)(2,1)}), bf16[3,2048,256]{2,1,0:T(8,128)(2,1)}) %all-gather.2.cloned.1.call-update) | async-done | bytes 3145744 | tf_op jit(solution)/shard_map/all_gather | solution.py:199
  140.4 5.1 %convert_element_type.418 = f32[3,2048,256]{2,1,0:T(8,128)} convert(bf16[3,2048,256]{2,1,0:T(8,128)(2,1)} %all-gather.2.cloned.1.call-done) | non-fusion elementwise | flops 1572864 | bytes 9437184 | tf_op jit(solution)/shard_map/convert_element_type | solution.py:201
  145.4 5.9 %while.1 = (s32[]{:T(128)}, f32[3,2048,256]{2,1,0:T(8,128)}, s32[2,3]{1,0:T(2,128)S(1)}, f32[2,3,64,64]{3,2,1,0:T(8,128)S(1)}, s32[]{:T(128)}) while((s32[]{:T(128)}, f32[3,2048,256]{2,1,0:T(8,128)}, s32[2,3]{1,0:T(2,128)S(1)}, f32[2,3,64,64]{3,2,1,0:T(8,128)S(1)}, s32[]{:T(128)}) %tuple.62), condition=%wide.while_cond, body=%wide.while_body.sunk | while | flops 2 | bytes 147581 | solution.py:204
  146.1 2.3 bitcast_dynamic-update-slice_fusion.2
  149.0 2.3 bitcast_dynamic-update-slice_fusion.2
  153.2 3.9 %fusion.8 = f32[2,64,128,128]{3,2,1,0:T(8,128)S(1)} fusion(bf16[2,1,64,128,128]{4,3,2,1,0:T(8,128)(2,1)} %param.7, f32[128,128]{1,0:T(8,128)S(1)} %get-tuple-element.89, f32[64]{0:T(128)S(1)} %fusion.158, f32[2,128,128]{2,1,0:T(8,128)S(1)} %copy.134, f32[128,128]{1,0:T(8,128)S(1)} %get-tuple-element.88), kind=kLoop, calls=%fused_computation.23 | loop fusion | flops 16777216 | bytes 12845312 | tf_op jit(solution)/shard_map/vmap()/add | solution.py:78
  157.3 7.7 %fusion.247 = (f32[2,64,128,1]{3,2,1,0:T(8,128)}, f32[2,64,128,1]{3,2,1,0:T(8,128)}) fusion(f32[2,64,128,128]{3,2,1,0:T(8,128)S(1)} %fusion.8), kind=kLoop, calls=%fused_computation.372 | loop fusion | bytes 262144 | tf_op jit(solution)/shard_map/vmap(jit(_pad))/slice | solution.py:52
  166.1 5.4 %broadcast_multiply_fusion.1 = (f32[2,64,128,128]{3,2,1,0:T(8,128)}, f32[2,64,128,128]{3,2,1,0:T(8,128)S(1)}) fusion(f32[64]{0:T(128)S(1)} %multiply_exponential_fusion, f32[2,128,128]{2,1,0:T(8,128)S(1)} %copy.137, f32[2,128,128]{2,1,0:T(8,128)S(1)} %copy.139), kind=kLoop, calls=%fused_computation.26 | loop fusion | flops 4194304 | bytes 17039616 | tf_op jit(solution)/shard_map/vmap()/mul | solution.py:80
  171.5 3.2 copy-done.1
  174.9 13.3 %fusion.246 = (f32[2,64,128,1]{3,2,1,0:T(8,128)}, f32[2,64,128,1]{3,2,1,0:T(8,128)}) fusion(f32[2,64,128,128]{3,2,1,0:T(8,128)} %get-tuple-element.86), kind=kLoop, calls=%fused_computation.371 | loop fusion | bytes 262144 | tf_op jit(solution)/shard_map/vmap(jit(_pad))/slice | solution.py:53
  188.2 12.6 %fusion.3 = f32[2,64,129,128]{3,2,1,0:T(8,128)} fusion(f32[2,64,128,128]{3,2,1,0:T(8,128)S(1)} %bitcast.266, f32[2,64,1,128]{3,2,1,0:T(1,128)S(1)} %get-tuple-element.56, f32[2,64,1,128]{3,2,1,0:T(1,128)S(1)} %get-tuple-element.55, f32[2,64,1,128]{3,2,1,0:T(1,128)S(1)} %get-tuple-element.54, f32[2,64,128,128]{3,2,1,0:T(8,128)} %copy-done.1, ...), kind=kLoop, calls=%fused_computation.14 | loop fusion | flops 23248896 | bytes 25493504 | tf_op jit(solution)/shard_map/vmap()/add | solution.py:61
  200.8 25.9 %fusion.1 = f32[2,64,128,129]{3,2,1,0:T(8,128)} fusion(f32[2,64,128,128]{3,2,1,0:T(8,128)S(1)} %bitcast.266, f32[2,64,128,1]{3,2,1,0:T(8,128)} %get-tuple-element.52, f32[2,64,128,1]{3,2,1,0:T(8,128)} %get-tuple-element.51, f32[2,64,128,1]{3,2,1,0:T(8,128)} %get-tuple-element.50, f32[2,64,128,128]{3,2,1,0:T(8,128)} %get-tuple-element.86, ...), kind=kLoop, calls=%fused_computation.9 | loop fusion | flops 23248896 | bytes 25493504 | tf_op jit(solution)/shard_map/vmap()/add | solution.py:61
  226.7 22.0 %convert_bitcast_fusion = (bf16[2,1,64,128,128]{4,3,2,1,0:T(8,128)(2,1)}, f32[2,64,128,128]{3,2,1,0:T(8,128)}) fusion(f32[2,64,129,128]{3,2,1,0:T(8,128)} %fusion.3, f32[2,64,128,129]{3,2,1,0:T(8,128)} %fusion.1, bf16[2,1,64,128,128]{4,3,2,1,0:T(8,128)(2,1)} %param.7, f32[128,128]{1,0:T(8,128)S(1)} %get-tuple-element.89, f32[64]{0:T(128)S(1)} %fusion.158, ...), kind=kLoop, calls=%fused_computation.24 | loop fusion | flops 31457280 | bytes 50594048 | tf_op jit(solution)/shard_map/broadcast_in_dim | solution.py:244
  248.7 3.8 %reduce_sum.29 = f32[2,128,128]{2,1,0:T(8,128)S(1)} reduce(f32[2,64,128,128]{3,2,1,0:T(8,128)} %get-tuple-element.44, f32[]{:T(128)} %constant.206.clone.1), dimensions={1}, to_apply=%region_1.2 | reduce | flops 2064384 | bytes 8519684 | tf_op jit(solution)/shard_map/vmap()/reduce_sum | solution.py:86
  252.5 9.8 %add.542 = f32[2,64,2,64,2]{4,3,2,1,0:T(8,128)} reshape(f32[2,128,128]{2,1,0:T(8,128)S(1)} %multiply_add_fusion) | data formatting | bytes 262144 | tf_op jit(solution)/shard_map/vmap()/add | solution.py:86
  262.3 4.5 %reduce_sum.30 = f32[2,64,64]{2,1,0:T(8,128)S(1)} reduce(f32[2,64,2,64,2]{4,3,2,1,0:T(8,128)} %add.542, f32[]{:T(128)} %constant.206.clone.1), dimensions={2,4}, to_apply=%region_2.3 | reduce | flops 24576 | bytes 163844 | tf_op jit(solution)/shard_map/vmap()/reduce_sum | solution.py:87
  267.0 17.1 %all_gather.7 = bf16[2,16,4096]{2,0,1:T(2,128)(2,1)S(1)} all-gather(bf16[2,1,4096]{2,0,1:T(2,128)(2,1)S(1)} %convert_element_type.422), channel_id=1, replica_groups=mesh['wide'=16,'grp'=8] {'wide'}, dimensions={1}, use_global_device_ids=true | all-gather | bytes 278528 | tf_op jit(solution)/shard_map/all_gather | solution.py:214
  285.3 6.6 %collective-permute-start = (bf16[16,256]{1,0:T(8,128)(2,1)S(1)}, bf16[16,256]{1,0:T(8,128)(2,1)S(1)}, u32[]{:S(2)}, u32[]{:S(2)}) collective-permute-start(bf16[16,256]{1,0:T(8,128)(2,1)S(1)} %get-tuple-element.84), channel_id=1, source_target_pairs={{0,1},{1,0},{2,3},{3,2},{4,5},{5,4},{6,7},{7,6},{8,9},{9,8},{10,11... | collective-permute-start | bytes 24584 | tf_op jit(solution)/shard_map/ppermute | solution.py:33
  292.4 2.3 collective-permute-start.6
  295.0 2.1 collective-permute-start.4
  297.1 1.5 collective-permute-start.3
  298.7 2.8 collective-permute-done.1
  301.5 1.3 collective-permute-start.2
  302.7 2.0 collective-permute-done.2
  309.1 1.5 reshape.554
  310.7 6.5 %all-to-all-start.2 = ((bf16[128,2,256]{2,1,0:T(2,128)(2,1)}), bf16[128,2,256]{2,1,0:T(2,128)(2,1)S(1)}, u32[]{:S(2)}, u32[]{:S(2)}) async-start(bf16[128,2,256]{2,1,0:T(2,128)(2,1)} %reshape.554), calls=%async_computation.2 | async-start | bytes 262144 | tf_op jit(solution)/shard_map/all_to_all | solution.py:241
  317.8 9.3 %all-to-all-done.2 = bf16[128,2,256]{2,1,0:T(2,128)(2,1)S(1)} async-done(((bf16[128,2,256]{2,1,0:T(2,128)(2,1)}), bf16[128,2,256]{2,1,0:T(2,128)(2,1)S(1)}, u32[]{:S(2)}, u32[]{:S(2)}) %all-to-all-start.2) | async-done | bytes 131104 | tf_op jit(solution)/shard_map/all_to_all | solution.py:241
  327.8 2.0 copy.162
  329.9 1.1 copy.150
  331.8 1.1 copy.151
  (165 shorter events, 31.5 us)
Async XLA Ops:
  7.2 133.2 %all-gather.2.cloned.1.call-start = ((), (), s32[]{:S(2)}) async-start(), calls=%async_computation.3 | async-start | bytes 3342336 | tf_op jit(solution)/shard_map/all_gather | solution.py:199
  7.3 6.4 %copy-start.3 = (f32[32,64]{1,0:T(8,128)}, f32[32,64]{1,0:T(8,128)S(1)}, u32[]{:S(2)}) copy-start(f32[32,64]{1,0:T(8,128)S(1)} %get-tuple-element.98) | copy-start | bytes 24580
  62.3 7.6 %copy-start.2 = (bf16[3,16,128,16]{1,2,3,0:T(8,128)(2,1)S(1)}, bf16[3,16,128,16]{1,2,3,0:T(8,128)(2,1)}, u32[]{:S(2)}) copy-start(bf16[3,16,128,16]{1,2,3,0:T(8,128)(2,1)} %get-tuple-element.57) | copy-start | bytes 589828
  69.9 6.8 %copy-start.4 = (f32[32,64]{1,0:T(8,128)S(1)}, f32[32,64]{1,0:T(8,128)}, u32[]{:S(2)}) copy-start(f32[32,64]{1,0:T(8,128)} %copy-done.3) | copy-start | bytes 24580
  76.7 19.6 %copy-start.8 = (s32[256]{0:T(256)S(1)}, s32[256]{0:T(256)}, u32[]{:S(2)}) copy-start(s32[256]{0:T(256)} %param.6) | copy-start | bytes 3076
  151.3 0.7 copy-start.5
  157.2 8.4 %copy-start = (f32[2,64,128,128]{3,2,1,0:T(8,128)}, f32[2,64,128,128]{3,2,1,0:T(8,128)S(1)}, u32[]{:S(2)}) copy-start(f32[2,64,128,128]{3,2,1,0:T(8,128)S(1)} %fusion.8) | copy-start | bytes 25165828
  166.1 22.1 %slice-start = ((s8[8388608]{0:T(1024)(128)(4,1)}), s8[4194304]{0:T(1024)(128)(4,1)S(1)}, s32[]{:S(2)}) async-start(s8[8388608]{0:T(1024)(128)(4,1)} %bitcast.265), calls=%async_computation.4 | async-start | bytes 8388608
  171.5 3.2 copy-start.1
  174.9 13.3 %slice-start.1 = ((s8[8388608]{0:T(1024)(128)(4,1)}), s8[4194304]{0:T(1024)(128)(4,1)S(1)}, s32[]{:S(2)}) async-start(s8[8388608]{0:T(1024)(128)(4,1)} %bitcast.265), calls=%async_computation.5 | async-start | bytes 8388608
  252.5 32.5 %copy-start.7 = (pred[2,4]{1,0:T(4,128)(4,1)S(1)}, pred[2,4]{1,0:T(4,128)(4,1)}, u32[]{:S(2)}) copy-start(pred[2,4]{1,0:T(4,128)(4,1)} %broadcast_in_dim.29) | copy-start | bytes 28
  262.3 43.6 %copy-start.6 = (f32[32,64]{1,0:T(8,128)S(1)}, f32[32,64]{1,0:T(8,128)}, u32[]{:S(2)}) copy-start(f32[32,64]{1,0:T(8,128)} %get-tuple-element.101) | copy-start | bytes 24580
  285.3 13.3 %collective-permute-start = (bf16[16,256]{1,0:T(8,128)(2,1)S(1)}, bf16[16,256]{1,0:T(8,128)(2,1)S(1)}, u32[]{:S(2)}, u32[]{:S(2)}) collective-permute-start(bf16[16,256]{1,0:T(8,128)(2,1)S(1)} %get-tuple-element.84), channel_id=1, source_target_pairs={{0,1},{1,0},{2,3},{3,2},{4,5},{5,4},{6,7},{7,6},{8,9},{9,8},{10,11... | collective-permute-start | bytes 24584 | tf_op jit(solution)/shard_map/ppermute | solution.py:33
  292.4 12.4 %collective-permute-start.6 = (bf16[16,256]{1,0:T(8,128)(2,1)S(1)}, bf16[16,256]{1,0:T(8,128)(2,1)S(1)}, u32[]{:S(2)}, u32[]{:S(2)}) collective-permute-start(bf16[16,256]{1,0:T(8,128)(2,1)S(1)} %get-tuple-element.78), channel_id=1, source_target_pairs={{0,7},{1,6},{2,5},{3,4},{4,3},{5,2},{6,1},{7,0},{8,15},{9,14},{10,... | collective-permute-start | bytes 24584 | tf_op jit(solution)/shard_map/ppermute | solution.py:33
  294.7 10.0 %collective-permute-start.5 = (bf16[16,256]{1,0:T(8,128)(2,1)S(1)}, bf16[16,256]{1,0:T(8,128)(2,1)S(1)}, u32[]{:S(2)}, u32[]{:S(2)}) collective-permute-start(bf16[16,256]{1,0:T(8,128)(2,1)S(1)} %get-tuple-element.79), channel_id=1, source_target_pairs={{0,6},{1,7},{2,4},{3,5},{4,2},{5,3},{6,0},{7,1},{8,14},{9,15},{10,... | collective-permute-start | bytes 24584 | tf_op jit(solution)/shard_map/ppermute | solution.py:33
  295.0 9.7 %collective-permute-start.4 = (bf16[16,256]{1,0:T(8,128)(2,1)S(1)}, bf16[16,256]{1,0:T(8,128)(2,1)S(1)}, u32[]{:S(2)}, u32[]{:S(2)}) collective-permute-start(bf16[16,256]{1,0:T(8,128)(2,1)S(1)} %get-tuple-element.80), channel_id=1, source_target_pairs={{0,5},{1,4},{2,7},{3,6},{4,1},{5,0},{6,3},{7,2},{8,13},{9,12},{10,... | collective-permute-start | bytes 24584 | tf_op jit(solution)/shard_map/ppermute | solution.py:33
  297.1 7.6 %collective-permute-start.3 = (bf16[16,256]{1,0:T(8,128)(2,1)S(1)}, bf16[16,256]{1,0:T(8,128)(2,1)S(1)}, u32[]{:S(2)}, u32[]{:S(2)}) collective-permute-start(bf16[16,256]{1,0:T(8,128)(2,1)S(1)} %get-tuple-element.81), channel_id=1, source_target_pairs={{0,4},{1,5},{2,6},{3,7},{4,0},{5,1},{6,2},{7,3},{8,12},{9,13},{10,... | collective-permute-start | bytes 24584 | tf_op jit(solution)/shard_map/ppermute | solution.py:33
  298.7 2.8 collective-permute-start.1
  301.5 3.2 collective-permute-start.2
  310.7 16.4 %all-to-all-start.2 = ((bf16[128,2,256]{2,1,0:T(2,128)(2,1)}), bf16[128,2,256]{2,1,0:T(2,128)(2,1)S(1)}, u32[]{:S(2)}, u32[]{:S(2)}) async-start(bf16[128,2,256]{2,1,0:T(2,128)(2,1)} %reshape.554), calls=%async_computation.2 | async-start | bytes 262144 | tf_op jit(solution)/shard_map/all_to_all | solution.py:241
Sparse Core Ops, SparseCore 0:
  96.4 43.9 all-gather.1
